TPU v7x, 256 devices: a whole 4x4x8 slice. The times are simulated.
256 devices in a mesh: wide: 32 (over x, z), narrow: 8 (over y, core).
Axes of the slice: x: 4, y: 4, z: 8, core: 2. Of those that a mesh axis runs over, the one named last changes fastest.
Arguments:
- panel_loads: float32 [2, 2048, 256], P(None, 'narrow'), may hold values from -6 to 6
- tail_loads: float32 [98304, 256], P(('narrow', 'wide')), may hold values from -6 to 6
- inverses: float32 [2, 2048, 2048], P(None, 'wide', 'narrow'), may hold values from -0.125 to 0.125
- cross_factor: float32 [2048, 2048], P('wide', 'narrow'), may hold values from -0.125 to 0.125
- tail_factor: float32 [2, 2048, 98304], P(None, 'wide', 'narrow'), may hold values from -0.1875 to 0.1875
Outputs:
- solution: float32 [2, 2048, 256], P(None, 'wide')
- tail_rest: float32 [98304, 256], P(('narrow', 'wide'))
All inputs are finite; a program needn't handle non-finite values.
Results may differ from a plain program's by a relative error of at most 0.000082.
Values sent between devices are 32-bit elements; how exact they have to be, the bound alone decides.
A program may use at most 128 MiB of HBM per device.

v0:
```python
import jax
import jax.numpy as jnp
from jax import lax
from jax.sharding import PartitionSpec as P


def contract(factor, values):
    return lax.dot_general(
        factor,
        values,
        (((0,), (0,)), ((), ())),
        precision=lax.Precision.HIGHEST,
        preferred_element_type=jnp.float32,
    )


def solve_panel(inverse, rhs):
    partial_value = jnp.dot(
        inverse, rhs, precision=lax.Precision.HIGHEST, preferred_element_type=jnp.float32
    )
    return lax.psum(partial_value, "narrow")


def carry_over(cross_factor, first):
    return lax.psum(contract(cross_factor, first), "wide")


def on_device(panel_loads, tail_loads, inverses, cross_factor, tail_factor):

    def panel_term(index, values):
        block = tail_factor[index]
        return contract(block, values)

    first = solve_panel(inverses[0], panel_loads[0])
    carried = carry_over(cross_factor, first)
    second = solve_panel(inverses[1], panel_loads[1] - carried)
    update = lax.psum_scatter(
        panel_term(0, first) + panel_term(1, second), "wide", scatter_dimension=0, tiled=True
    )
    solution = jnp.stack([first, second])
    return (solution, tail_loads - update)


def solution(mesh):
    in_specs = (
        P(None, "narrow", None),
        P(("narrow", "wide"), None),
        P(None, "wide", "narrow"),
        P("wide", "narrow"),
        P(None, "wide", "narrow"),
    )
    out_specs = (P(None, "wide", None), P(("narrow", "wide"), None))
    return jax.shard_map(
        on_device, mesh=mesh, in_specs=in_specs, out_specs=out_specs, check_vma=False
    )
```

profile of v0, /device:TPU:1, one launch (start us, length us, event | category | flops | bytes accessed | tf_op | source)
XLA Modules:
  0.0 548.3 jit_solution(18108480025359776959)
XLA Ops:
  7.2 0.0 copy-start
  7.2 0.0 all-reduce.4.cloned.1.call-start
  7.2 1.9 fusion.6
  9.1 0.0 all-reduce.4.cloned.1.call-update
  9.1 0.0 all-reduce.6.cloned.1.call-start
  9.2 67.4 %all-reduce.4.cloned.1.call-done = f32[64,256]{1,0:T(8,128)} async-done(((f32[64,256]{1,0:T(8,128)}), f32[64,256]{1,0:T(8,128)}) %all-reduce.4.cloned.1.call-update) | async-done | bytes 65552 | tf_op jit(solution)/shard_map/psum | solution.py:21
  76.5 0.0 copy-done
  76.5 2.0 convolution_bitcast_fusion
  78.5 0.0 all-reduce.6.cloned.1.call-update
  78.5 0.0 all-reduce.8.cloned.1.call-start
  78.6 143.0 %all-reduce.6.cloned.1.call-done = f32[256,256]{1,0:T(8,128)} async-done(((f32[256,256]{1,0:T(8,128)}), f32[256,256]{1,0:T(8,128)}) %all-reduce.6.cloned.1.call-update) | async-done | bytes 262160 | tf_op jit(solution)/shard_map/psum | solution.py:25
  221.6 2.0 convolution_bitcast_fusion.1
  223.5 0.0 all-reduce.8.cloned.1.call-update
  223.6 0.0 reduce-scatter.2.cloned.1.call-start
  223.6 13.7 %fusion.2 = f32[256,12288]{1,0:T(8,128)} fusion(f32[64,256]{1,0:T(8,128)} %all-reduce.4.cloned.1.call-done, f32[2,64,12288]{2,1,0:T(8,128)} %param.9), kind=kOutput, calls=%fused_computation.3 | convolution fusion | flops 2415919104 | bytes 15794176 | tf_op jit(solution)/shard_map/dot_general | solution.py:8
  237.4 50.5 %all-reduce.8.cloned.1.call-done = f32[64,256]{1,0:T(8,128)} async-done(((f32[64,256]{1,0:T(8,128)}), f32[64,256]{1,0:T(8,128)}) %all-reduce.8.cloned.1.call-update) | async-done | bytes 65552 | tf_op jit(solution)/shard_map/psum | solution.py:21
  287.8 16.2 %fusion = f32[12288,256]{0,1:T(8,128)} fusion(f32[256,12288]{1,0:T(8,128)} %fusion.2, f32[64,256]{1,0:T(8,128)} %all-reduce.8.cloned.1.call-done, f32[2,64,12288]{2,1,0:T(8,128)} %param.9), kind=kOutput, calls=%fused_computation.1 | convolution fusion | flops 2419064832 | bytes 28377088 | tf_op jit(solution)/shard_map/dot_general | solution.py:8
  304.0 0.0 copy-start.2
  304.0 0.0 copy-start.1
  304.0 0.0 copy-start.3
  304.0 0.0 reduce-scatter.2.cloned.1.call-update
  304.0 1.0 copy-done.2
  305.0 0.2 copy.7
  305.2 0.0 copy-done.1
  305.2 0.0 copy-done.3
  305.2 0.7 pad_maximum_fusion
  305.9 233.9 %reduce-scatter.2.cloned.1.call-done = f32[384,256]{0,1:T(8,128)} async-done(((f32[12288,256]{0,1:T(8,128)}), f32[384,256]{0,1:T(8,128)}) %reduce-scatter.2.cloned.1.call-update) | async-done | bytes 393232 | tf_op jit(solution)/shard_map/reduce_scatter | solution.py:37
  539.8 1.0 sub.7
  540.8 0.9 copy.8
Async XLA Ops:
  7.2 69.4 %copy-start = (f32[64,256]{1,0:T(8,128)S(1)}, f32[64,256]{1,0:T(8,128)}, u32[]{:S(2)}) copy-start(f32[64,256]{1,0:T(8,128)} %param.8) | copy-start | bytes 196612
  7.2 69.3 %all-reduce.4.cloned.1.call-start = ((), (), s32[]{:S(2)}) async-start(), calls=%async_computation.1 | async-start | bytes 131072 | tf_op jit(solution)/shard_map/psum | solution.py:21
  9.1 212.5 %all-reduce.6.cloned.1.call-start = ((), (), s32[]{:S(2)}) async-start(), calls=%async_computation.2 | async-start | bytes 524288 | tf_op jit(solution)/shard_map/psum | solution.py:25
  78.5 209.3 %all-reduce.8.cloned.1.call-start = ((), (), s32[]{:S(2)}) async-start(), calls=%async_computation.3 | async-start | bytes 131072 | tf_op jit(solution)/shard_map/psum | solution.py:21
  223.6 316.2 %reduce-scatter.2.cloned.1.call-start = ((), (), s32[]{:S(2)}) async-start(), calls=%async_computation.4 | async-start | bytes 12976128 | tf_op jit(solution)/shard_map/reduce_scatter | solution.py:37
  304.0 1.0 copy-start.2
  304.0 1.2 copy-start.1
  304.0 1.2 copy-start.3
Sparse Core Ops, SparseCore 0:
  10.9 65.5 all-reduce.3
  80.9 140.5 all-reduce.5
  224.6 63.2 all-reduce.7
  304.2 235.5 reduce-scatter.1
where the time goes:
time: 552 us; the launch traced here: 548 us
  waiting for transfers between devices  495 us (90%)
  matrix products  35.7 us (6%)
  between operations  13.8 us (2%)
    reduce_scatter x1, waiting for transfers between devices, on_device(): lax.psum_scatter(panel_term(0, first) + panel_term(1, second), 'wide', sc...  234 us
    psum x1, waiting for transfers between devices, carry_over(): return lax.psum(contract(cross_factor, first), 'wide')  143 us
    psum x2, waiting for transfers between devices, solve_panel(): return lax.psum(partial_value, 'narrow')  118 us
    dot_general x3, matrix products, contract(): lax.dot_general(factor, values, (((0,), (0,)), ((), ())), precision=lax.P...  31.9 us
  transfers between devices with their start and end apart: 4, of which 4 were waited for; matrix products, arithmetic and copies ran while one was open for 3% of the time, Pallas kernels for 0%

commit v1 on v0

v1 whole, which is shorter than its diff:
```python
import functools

import jax
import jax.numpy as jnp
from jax import lax
from jax.experimental import pallas as pl
from jax.experimental.pallas import tpu as pltpu
from jax.sharding import PartitionSpec as P

MESH = pl.DeviceIdType.MESH
NX, NZ, NY = 4, 8, 4
NW = NX * NZ
ROWS = 384
R1 = 256
R2 = 128
HIGH = lax.Precision.HIGHEST
F32 = jnp.float32
BF16 = jnp.bfloat16


def dot(a, b):
    return jnp.dot(a, b, precision=HIGH, preferred_element_type=F32)


def split(a):
    hi = a.astype(BF16)
    return hi, (a - hi.astype(F32)).astype(BF16)


def dot3(xh, xl, a):
    ah, al = split(a)
    out = jnp.dot(xh, ah, preferred_element_type=F32)
    out += jnp.dot(xl, ah, preferred_element_type=F32)
    return out + jnp.dot(xh, al, preferred_element_type=F32)


def kernel(
    pl_ref, inv_ref, cross_ref, loads_ref, tail_ref,
    sol_ref, out_ref,
    part, corebuf, ybuf, xg, xz, cpart, crecv, restall,
    a1, a2, pb, qb, recv1, xr0, xr1, farsum, farrecv, xt,
    core_s, core_r, y_s, y_r, cg_s, cg_r, known,
    rs_s, rs_r, ag_s, ag_r, gx_s, gx_r, gz_s, gz_r,
    a1_s, a1_r, a1_l, a2_s, a2_r, a2_l,
    b1_s, b1_r, b2_s, b2_r, b3_s, b3_r,
):
    w = lax.axis_index("wide")
    n = lax.axis_index("narrow")
    x, z = w // NZ, w % NZ
    y, core = n // 2, n % 2

    def xpos(d):
        return (x + d + NX) % NX

    def zpos(d):
        return (z + d + NZ) % NZ

    def at_x(d):
        return (xpos(d) * NZ + z, n)

    def at_z(d):
        return (x * NZ + zpos(d), n)

    def at_y(d):
        return (w, ((y + d) % NY) * 2 + core)

    other = (w, y * 2 + 1 - core)

    def remote(src, dst, ssem, rsem, device):
        return pltpu.make_async_remote_copy(
            src_ref=src, dst_ref=dst, send_sem=ssem, recv_sem=rsem,
            device_id=device, device_id_type=MESH,
        )

    barrier = pltpu.get_barrier_semaphore()
    peers = [at_x(d) for d in (1, 2, 3)] + [at_z(d) for d in range(1, 8)]
    peers += [at_y(d) for d in (1, 2, 3)] + [other]
    for device in peers:
        pl.semaphore_signal(barrier, inc=1, device_id=device, device_id_type=MESH)

    def lanes1(xd, zd):
        return pl.ds(pl.multiple_of((xd * NZ + zd) * ROWS, 128), R1)

    def lanes2(xd, zd):
        return pl.ds(pl.multiple_of((xd * NZ + zd) * ROWS + R1, 128), R2)

    def own1(zd):
        return pltpu.make_async_copy(
            tail_ref.at[:, :, lanes1(x, zd)], a1.at[zd, x], a1_l.at[zd]
        )

    def own2(xd, far):
        zd = zpos(4 * far)
        return pltpu.make_async_copy(
            tail_ref.at[:, :, lanes2(xd, zd)],
            a2.at[far, 0, :, :, pl.ds(xd * R2, R2)], a2_l.at[far, xd],
        )

    for zd in range(NZ):
        own1(zd).start()
    for far in (0, 1):
        for xd in range(NX):
            own2(xd, far).start()

    def send1(d, zd):
        return remote(
            tail_ref.at[:, :, lanes1(xpos(d), zd)], a1.at[zd, x],
            a1_s.at[d, zd], a1_r.at[4 - d, zd], at_x(d),
        )

    def send2(i, xd, far):
        d = (1, -1, 2, -2)[i]
        zd = zpos(d + 4 * far)
        to = pl.ds(pl.multiple_of(xd * R2, R2), R2)
        if i < 2:
            src = tail_ref.at[:, :, lanes2(xd, zd)]
            dst = a2.at[far, 1 + i, :, :, to]
        else:
            src = tail_ref.at[far, :, lanes2(xd, zd)]
            dst = a2.at[far, 3, i - 2, :, to]
        return remote(src, dst, a2_s.at[i, far, xd], a2_r.at[i, far, xd], at_z(d))

    def each1(d, act):
        def body(zd, carry):
            act(send1(d, zd))
            return carry
        lax.fori_loop(0, NZ, body, 0)

    def each2(i, act):
        def body(xd, carry):
            for far in (0, 1):
                act(send2(i, xd, far))
            return carry
        lax.fori_loop(0, NX, body, 0)

    start = lambda copy: copy.start()
    sent = lambda copy: copy.wait_send()
    arrived = lambda copy: copy.wait_recv()

    crossT = cross_ref[...].T
    part[0] = dot(inv_ref[0], pl_ref[0])

    pl.semaphore_wait(barrier, len(peers))
    for d in (1, 2, 3):
        pl.semaphore_signal(known, inc=1, device_id=at_x(d), device_id_type=MESH)

    half = 32
    mine = pl.ds(pl.multiple_of(core * half, half), half)
    theirs = pl.ds(pl.multiple_of((1 - core) * half, half), half)

    def core_copy(p):
        return remote(part.at[p, theirs], corebuf.at[p], core_s.at[p], core_r.at[p], other)

    def y_copy(p, d):
        return remote(
            ybuf.at[p, y], ybuf.at[p, y], y_s.at[p, d], y_r.at[p, 4 - d], at_y(d)
        )

    def cg_copy(p):
        return remote(
            xg.at[x, p, mine], xg.at[x, p, mine], cg_s.at[p], cg_r.at[p], other
        )

    def gx_copy(p, d):
        return remote(
            xg.at[x, p], xg.at[x, p], gx_s.at[p, d], gx_r.at[p, 4 - d], at_x(d)
        )

    def gz_copy(p, i):
        d = (1, -1, 2, -2)[i]
        return remote(xg.at[x, p], xz.at[i, p], gz_s.at[p, i], gz_r.at[p, i], at_z(d))

    def sum_narrow(p, between):
        core_copy(p).start()
        between(0)
        core_copy(p).wait_recv()
        ybuf[p, y] = part[p, mine] + corebuf[p]
        for d in (2, 1, 3):
            y_copy(p, d).start()
        between(1)
        for d in (2, 1, 3):
            y_copy(p, d).wait_recv()
        xg[x, p, mine] = (ybuf[p, 0] + ybuf[p, 1]) + (ybuf[p, 2] + ybuf[p, 3])
        cg_copy(p).start()
        cg_copy(p).wait_recv()
        for d in (2, 1, 3):
            gx_copy(p, d).start()
        for i in (2, 3, 0, 1):
            gz_copy(p, i).start()
        sol_ref[p] = xg[x, p]

    def between_first(stage):
        if stage == 0:
            each1(2, start)
            each2(2, start)
            each2(3, start)
        else:
            each1(1, start)
            each1(3, start)
            each2(0, start)
            each2(1, start)

    sum_narrow(0, between_first)

    cpart[...] = dot(crossT, xg[x, 0])
    pl.semaphore_wait(known, 3)

    def rows_of(i):
        return pl.ds(pl.multiple_of(i * 8, 8), 8)

    def rs_copy(i):
        to = (w + i) % NW
        return remote(
            cpart.at[rows_of(to)], crecv.at[w], rs_s.at[i], rs_r.at[NW - i], (to, n)
        )

    def ag_copy(i):
        return remote(
            restall.at[rows_of(w)], restall.at[rows_of(w)], ag_s.at[i], ag_r.at[NW - i],
            ((w + i) % NW, n),
        )

    def each_peer(copy, act):
        def body(i, carry):
            act(copy(i))
            return carry
        lax.fori_loop(1, NW, body, 0)

    each_peer(rs_copy, start)
    crecv[w] = cpart[rows_of(w), :]
    each_peer(rs_copy, arrived)
    restall[rows_of(w), :] = pl_ref[1, rows_of(w), :] - jnp.sum(crecv[...], axis=0)
    each_peer(ag_copy, start)
    each_peer(ag_copy, arrived)

    part[1] = dot(inv_ref[1], restall[...])
    sum_narrow(1, lambda stage: None)

    for p in (0, 1):
        for d in (1, 2, 3):
            gx_copy(p, d).wait_recv()
        for i in range(4):
            gz_copy(p, i).wait_recv()

    def keep(which, value):
        hi, lo = split(value.T)
        xt[which, 0] = hi
        xt[which, 1] = lo

    keep(0, xg[...].reshape(512, 256))
    around = [xg[x].reshape(128, 256), xz[0].reshape(128, 256), xz[1].reshape(128, 256)]
    keep(1, jnp.concatenate(around + [xz[2, 0], xz[3, 0]], axis=0))
    keep(2, jnp.concatenate(around + [xz[2, 1], xz[3, 1]], axis=0))

    for i in range(4):
        each2(i, arrived)
    for far in (0, 1):
        for xd in range(NX):
            own2(xd, far).wait()

    def product2(far):
        value = dot3(xt[1 + far, 0], xt[1 + far, 1], a2[far].reshape(512, NX * R2))
        for xd in range(NX):
            qb[far, xd] = value[:, xd * R2:(xd + 1) * R2]

    H = (pl.ds(0, 128), pl.ds(128, 128))

    def x_first(far, way):
        return remote(
            qb.at[far, xpos(2), H[way]], xr0.at[far, way],
            b2_s.at[far, way, 0], b2_r.at[far, way, 0], at_x((1, -1)[way]),
        )

    def x_second(far, way):
        d = (1, -1)[way]
        return remote(
            qb.at[far, xpos(d)], xr1.at[far, way],
            b2_s.at[far, way, 1], b2_r.at[far, way, 1], at_x(d),
        )

    def z_copy(way, s, h):
        d = (-1, 1)[way]
        return remote(
            pb.at[zpos(d * (4 - s)), H[h]], recv1.at[way, s, H[h]],
            b1_s.at[way, s, h], b1_r.at[way, s, h], at_z(d),
        )

    def product1(d):
        zd = zpos(d)
        own1(zd).wait()
        for k in (1, 2, 3):
            send1(k, zd).wait_recv()
        pb[zd] = dot3(xt[0, 0], xt[0, 1], a1[zd].reshape(512, R1))

    def z_step(way, s):
        zd = zpos((-1, 1)[way] * (4 - s))
        halves = (way, 1 - way) if s == 1 else (way, 1 - way)
        for h in halves:
            if s > 1 or h == way:
                z_copy(way, s - 1, h).wait_recv()
                pb[zd, H[h], :] = pb[zd, H[h], :] + recv1[way, s - 1, H[h], :]
            z_copy(way, s, h).start()

    product1(4)
    z_copy(0, 0, 0).start()
    z_copy(1, 0, 1).start()
    product2(1)
    for way in (0, 1):
        x_first(1, way).start()
    product1(-3)
    product1(3)
    z_step(0, 1)
    z_step(1, 1)
    for way in (0, 1):
        x_first(1, way).wait_recv()
        spot = xpos((1, -1)[way])
        qb[1, spot, H[way], :] = qb[1, spot, H[way], :] + xr0[1, way]
        x_second(1, way).start()
    product2(0)
    for way in (0, 1):
        x_first(0, way).start()
    product1(-2)
    product1(2)
    z_step(0, 2)
    z_step(1, 2)
    for way in (0, 1):
        x_second(1, way).wait_recv()
    farsum[...] = qb[1, x] + (xr1[1, 0] + xr1[1, 1])
    far_copy = remote(farsum, farrecv, b3_s.at[0], b3_r.at[0], at_z(4))
    far_copy.start()
    for way in (0, 1):
        x_first(0, way).wait_recv()
        spot = xpos((1, -1)[way])
        qb[0, spot, H[way], :] = qb[0, spot, H[way], :] + xr0[0, way]
        x_second(0, way).start()
    product1(-1)
    product1(1)
    z_step(0, 3)
    z_step(1, 3)
    product1(0)
    for way in (0, 1):
        x_second(0, way).wait_recv()
    far_copy.wait_recv()
    total2 = qb[0, x] + (xr1[0, 0] + xr1[0, 1]) + farrecv[...]
    out_ref[R1:, :] = loads_ref[R1:, :] - total2.T
    for way in (0, 1):
        for h in (0, 1):
            z_copy(way, 3, h).wait_recv()
    total1 = pb[z] + (recv1[0, 3] + recv1[1, 3])
    out_ref[:R1, :] = loads_ref[:R1, :] - total1.T

    for p in (0, 1):
        core_copy(p).wait_send()
        cg_copy(p).wait_send()
        for d in (1, 2, 3):
            y_copy(p, d).wait_send()
            gx_copy(p, d).wait_send()
        for i in range(4):
            gz_copy(p, i).wait_send()
    each_peer(rs_copy, sent)
    each_peer(ag_copy, sent)
    for d in (1, 2, 3):
        each1(d, sent)
    for i in range(4):
        each2(i, sent)
    for far in (0, 1):
        for way in (0, 1):
            x_first(far, way).wait_send()
            x_second(far, way).wait_send()
    z_copy(0, 0, 0).wait_send()
    z_copy(1, 0, 1).wait_send()
    for way in (0, 1):
        for s in (1, 2, 3):
            for h in (0, 1):
                z_copy(way, s, h).wait_send()
    far_copy.wait_send()


def on_device(panel_loads, tail_loads, inverses, cross_factor, tail_factor):
    vmem = pl.BlockSpec(memory_space=pltpu.VMEM)
    dma = pltpu.SemaphoreType.DMA
    scratch = [
        pltpu.VMEM((2, 64, 256), F32),
        pltpu.VMEM((2, 32, 256), F32),
        pltpu.VMEM((2, NY, 32, 256), F32),
        pltpu.VMEM((NX, 2, 64, 256), F32),
        pltpu.VMEM((4, 2, 64, 256), F32),
        pltpu.VMEM((256, 256), F32),
        pltpu.VMEM((NW, 8, 256), F32),
        pltpu.VMEM((256, 256), F32),
        pltpu.VMEM((NZ, NX, 2, 64, R1), F32),
        pltpu.VMEM((2, 4, 2, 64, NX * R2), F32),
        pltpu.VMEM((NZ, 256, R1), F32),
        pltpu.VMEM((2, NX, 256, R2), F32),
        pltpu.VMEM((2, 4, 256, R1), F32),
        pltpu.VMEM((2, 2, 128, R2), F32),
        pltpu.VMEM((2, 2, 256, R2), F32),
        pltpu.VMEM((256, R2), F32),
        pltpu.VMEM((256, R2), F32),
        pltpu.VMEM((3, 2, 256, 512), BF16),
        dma((2,)), dma((2,)), dma((2, 4)), dma((2, 4)), dma((2,)), dma((2,)),
        pltpu.SemaphoreType.REGULAR,
        dma((NW,)), dma((NW,)), dma((NW,)), dma((NW,)),
        dma((2, 4)), dma((2, 4)), dma((2, 4)), dma((2, 4)),
        dma((4, NZ)), dma((4, NZ)), dma((NZ,)),
        dma((4, 2, NX)), dma((4, 2, NX)), dma((2, NX)),
        dma((2, 4, 2)), dma((2, 4, 2)), dma((2, 2, 2)), dma((2, 2, 2)), dma((1,)), dma((1,)),
    ]
    return pl.pallas_call(
        kernel,
        out_shape=(
            jax.ShapeDtypeStruct((2, 64, 256), F32),
            jax.ShapeDtypeStruct((ROWS, 256), F32),
        ),
        in_specs=[vmem, vmem, vmem, vmem, pl.BlockSpec(memory_space=pl.ANY)],
        out_specs=(vmem, vmem),
        scratch_shapes=scratch,
        compiler_params=pltpu.CompilerParams(
            collective_id=0, has_side_effects=True, vmem_limit_bytes=48 * 1024 * 1024
        ),
    )(panel_loads, inverses, cross_factor, tail_loads, tail_factor)


def solution(mesh):
    in_specs = (
        P(None, "narrow", None),
        P(("narrow", "wide"), None),
        P(None, "wide", "narrow"),
        P("wide", "narrow"),
        P(None, "wide", "narrow"),
    )
    out_specs = (P(None, "wide", None), P(("narrow", "wide"), None))
    return jax.shard_map(
        on_device, mesh=mesh, in_specs=in_specs, out_specs=out_specs, check_vma=False
    )
```

time: 552 us -> 125 us (0.23)
  waiting for transfers between devices: 495 us -> 0 us
  Pallas kernels: 0 us -> 118 us
  matrix products: 35.7 us -> 0 us
  between operations: 13.8 us -> 0.65 us
    psum x3 -> x0, waiting for transfers between devices: 261 us -> none  [the longest x1 143 us: carry_over(): return lax.psum(contract(cross_factor, first), 'wide')]
    reduce_scatter x1 -> x0, waiting for transfers between devices: 234 us -> none  [on_device(): lax.psum_scatter(panel_term(0, first) + panel_term(1, second), 'wide', sc...]
    pallas_call x0 -> x1, Pallas kernels: none -> 118 us  [on_device(): pl.pallas_call(kernel, out_shape=(jax.ShapeDtypeStruct((2, 64, 256), F32)...]
    dot_general x5 -> x0, matrix products: 35.7 us -> none  [the longest x3 31.9 us: contract(): lax.dot_general(factor, values, (((0,), (0,)), ((), ())), precision=lax.P...]
  transfers between devices with their start and end apart: 4 -> 0, of which waited for: 4 -> 0; matrix products, arithmetic and copies ran while one was open for 3% -> 0% of each run, Pallas kernels for 0% -> 0%
where the time goes in v1:
time: 125 us; the launch traced here: 124 us
  Pallas kernels  118 us (94%)
  local copies, waits for them, and re-layouts  5.18 us (4%)
    pallas_call x1, Pallas kernels, on_device(): pl.pallas_call(kernel, out_shape=(jax.ShapeDtypeStruct((2, 64, 256), F32)...  118 us
    unnamed x10, local copies, waits for them, and re-layouts  5.18 us

profile of v1, /device:TPU:1, one launch (start us, length us, event | category | flops | bytes accessed | tf_op | source)
XLA Modules:
  0.0 123.6 jit_solution(13663071228697680730)
XLA Ops:
  0.6 0.0 copy-start
  0.6 1.0 copy-done
  1.7 0.0 copy-start.1
  1.7 1.0 copy-done.1
  2.7 0.0 copy-start.2
  2.7 0.9 copy-done.2
  3.6 0.0 copy-start.3
  3.6 0.8 copy-done.3
  4.4 117.8 %shard_map.68 = (f32[2,64,256]{2,1,0:T(8,128)S(1)}, f32[384,256]{1,0:T(8,128)S(1)}) custom-call(f32[2,256,256]{2,1,0:T(8,128)S(1)} %copy-done, f32[2,64,256]{2,1,0:T(8,128)S(1)} %copy-done.2, f32[64,256]{1,0:T(8,128)S(1)} %copy-done.3, f32[384,256]{1,0:T(8,128)S(1)} %copy-done.1, f32[2,64,12288]{2,1,0:T(8,128)} %tail_ref.1), custom_call_target="tpu_custom_call" | custom-call | tf_op jit(solution)/shard_map/pallas_call | solution.py:409
  122.2 0.7 copy.9
  122.9 0.7 copy.10
Async XLA Ops:
  0.6 1.0 copy-start
  1.7 1.0 copy-start.1
  2.7 0.9 copy-start.2
  3.6 0.8 copy-start.3

commit v2 on v1

--- a/solution.py
+++ b/solution.py
@@ -16,6 +16,18 @@
 HIGH = lax.Precision.HIGHEST
 F32 = jnp.float32
 BF16 = jnp.bfloat16
+SCHEDULE = {
+    0: ((1, 0, 1),),
+    1: ((1, 1, 2), (2, 0, 1)),
+    2: (),
+    3: ((1, 2, 3), (2, 1, 2)),
+    4: ((1, 3, 4), (2, 2, 3)),
+    6: (),
+    7: ((1, 4, 5), (2, 3, 4)),
+    8: ((1, 5, 6),),
+    9: ((1, 6, 7),),
+    10: ((1, 7, 8),),
+}
 
 
 def dot(a, b):
@@ -35,14 +47,15 @@
 
 
 def kernel(
-    pl_ref, inv_ref, cross_ref, loads_ref, tail_ref,
+    pl_hbm, inv_hbm, cross_hbm, loads_hbm, tail_ref,
     sol_ref, out_ref,
+    pl_ref, inv_ref, cross_ref, loads_ref,
     part, corebuf, ybuf, xg, xz, cpart, crecv, restall,
     a1, a2, pb, qb, recv1, xr0, xr1, farsum, farrecv, xt,
     core_s, core_r, y_s, y_r, cg_s, cg_r, known,
-    rs_s, rs_r, ag_s, ag_r, gx_s, gx_r, gz_s, gz_r,
+    rs_s, rs_r, ag_s, ag_r, gx_s, gx_r, gz_s, gz_r, fx_s, fx_r, fz_s, fz_r,
     a1_s, a1_r, a1_l, a2_s, a2_r, a2_l,
-    b1_s, b1_r, b2_s, b2_r, b3_s, b3_r,
+    b1_s, b1_r, b2_s, b2_r, b3_s, b3_r, load,
 ):
     w = lax.axis_index("wide")
     n = lax.axis_index("narrow")
@@ -73,11 +86,20 @@
         )
 
     barrier = pltpu.get_barrier_semaphore()
-    peers = [at_x(d) for d in (1, 2, 3)] + [at_z(d) for d in range(1, 8)]
+    peers = [at_x(d) for d in (1, 2, 3)] + [at_z(d) for d in (1, -1, 2, -2)]
     peers += [at_y(d) for d in (1, 2, 3)] + [other]
     for device in peers:
         pl.semaphore_signal(barrier, inc=1, device_id=device, device_id_type=MESH)
 
+    loads = [
+        pltpu.make_async_copy(src, dst, load.at[i])
+        for i, (src, dst) in enumerate((
+            (pl_hbm, pl_ref), (inv_hbm, inv_ref), (cross_hbm, cross_ref), (loads_hbm, loads_ref),
+        ))
+    ]
+    for copy in loads:
+        copy.start()
+
     def lanes1(xd, zd):
         return pl.ds(pl.multiple_of((xd * NZ + zd) * ROWS, 128), R1)
 
@@ -86,25 +108,19 @@
 
     def own1(zd):
         return pltpu.make_async_copy(
-            tail_ref.at[:, :, lanes1(x, zd)], a1.at[zd, x], a1_l.at[zd]
+            tail_ref.at[:, :, lanes1(x, zd)], a1.at[zd, :, x], a1_l.at[zd]
         )
 
     def own2(xd, far):
         zd = zpos(4 * far)
         return pltpu.make_async_copy(
             tail_ref.at[:, :, lanes2(xd, zd)],
-            a2.at[far, 0, :, :, pl.ds(xd * R2, R2)], a2_l.at[far, xd],
-        )
-
-    for zd in range(NZ):
-        own1(zd).start()
-    for far in (0, 1):
-        for xd in range(NX):
-            own2(xd, far).start()
+            a2.at[far, 0, :, :, pl.ds(pl.multiple_of(xd * R2, R2), R2)], a2_l.at[far, xd],
+        )
 
     def send1(d, zd):
         return remote(
-            tail_ref.at[:, :, lanes1(xpos(d), zd)], a1.at[zd, x],
+            tail_ref.at[:, :, lanes1(xpos(d), zd)], a1.at[zd, :, x],
             a1_s.at[d, zd], a1_r.at[4 - d, zd], at_x(d),
         )
 
@@ -120,6 +136,28 @@
             dst = a2.at[far, 3, i - 2, :, to]
         return remote(src, dst, a2_s.at[i, far, xd], a2_r.at[i, far, xd], at_z(d))
 
+    def feed1(first, last):
+        def body(i, carry):
+            zd = zpos((4 - (i + 1) // 2) * (1 - 2 * (i % 2)))
+            for d in (2, 1, 3):
+                send1(d, zd).start()
+            own1(zd).start()
+            return carry
+        lax.fori_loop(first, last, body, 0)
+
+    def feed2(first, last):
+        def body(xd, carry):
+            for far in (1, 0):
+                for i in (2, 3, 0, 1):
+                    send2(i, xd, far).start()
+                own2(xd, far).start()
+            return carry
+        lax.fori_loop(first, last, body, 0)
+
+    def feed(stage):
+        for kind, first, last in SCHEDULE[stage]:
+            (feed1 if kind == 1 else feed2)(first, last)
+
     def each1(d, act):
         def body(zd, carry):
             act(send1(d, zd))
@@ -137,12 +175,14 @@
     sent = lambda copy: copy.wait_send()
     arrived = lambda copy: copy.wait_recv()
 
+    for copy in loads:
+        copy.wait()
     crossT = cross_ref[...].T
     part[0] = dot(inv_ref[0], pl_ref[0])
 
     pl.semaphore_wait(barrier, len(peers))
     for d in (1, 2, 3):
-        pl.semaphore_signal(known, inc=1, device_id=at_x(d), device_id_type=MESH)
+        pl.semaphore_signal(known.at[0], inc=1, device_id=at_x(d), device_id_type=MESH)
 
     half = 32
     mine = pl.ds(pl.multiple_of(core * half, half), half)
@@ -163,100 +203,122 @@
 
     def gx_copy(p, d):
         return remote(
-            xg.at[x, p], xg.at[x, p], gx_s.at[p, d], gx_r.at[p, 4 - d], at_x(d)
+            xg.at[x, p, mine], xg.at[x, p, mine], gx_s.at[p, d], gx_r.at[p, 4 - d], at_x(d)
         )
 
     def gz_copy(p, i):
         d = (1, -1, 2, -2)[i]
-        return remote(xg.at[x, p], xz.at[i, p], gz_s.at[p, i], gz_r.at[p, i], at_z(d))
-
-    def sum_narrow(p, between):
+        return remote(
+            xg.at[x, p, mine], xz.at[i, p, mine], gz_s.at[p, i], gz_r.at[p, i], at_z(d)
+        )
+
+    def fx_copy(p, d):
+        return remote(
+            xg.at[xpos(d), p, mine], xg.at[xpos(d), p, mine],
+            fx_s.at[p, d], fx_r.at[p, d], other,
+        )
+
+    def fz_copy(p, i):
+        return remote(
+            xz.at[i, p, mine], xz.at[i, p, mine], fz_s.at[p, i], fz_r.at[p, i], other
+        )
+
+    def pass_on(p):
+        for d in (1, 3, 2):
+            gx_copy(p, 4 - d).wait_recv()
+            fx_copy(p, d).start()
+        for i in range(4):
+            gz_copy(p, i).wait_recv()
+            fz_copy(p, i).start()
+
+    def sum_narrow(p):
         core_copy(p).start()
-        between(0)
+        feed(6 * p)
         core_copy(p).wait_recv()
         ybuf[p, y] = part[p, mine] + corebuf[p]
         for d in (2, 1, 3):
             y_copy(p, d).start()
-        between(1)
+        feed(6 * p + 1)
         for d in (2, 1, 3):
             y_copy(p, d).wait_recv()
         xg[x, p, mine] = (ybuf[p, 0] + ybuf[p, 1]) + (ybuf[p, 2] + ybuf[p, 3])
         cg_copy(p).start()
-        cg_copy(p).wait_recv()
         for d in (2, 1, 3):
             gx_copy(p, d).start()
         for i in (2, 3, 0, 1):
             gz_copy(p, i).start()
-        sol_ref[p] = xg[x, p]
-
-    def between_first(stage):
-        if stage == 0:
-            each1(2, start)
-            each2(2, start)
-            each2(3, start)
-        else:
-            each1(1, start)
-            each1(3, start)
-            each2(0, start)
-            each2(1, start)
-
-    sum_narrow(0, between_first)
+        feed(6 * p + 2)
+        cg_copy(p).wait_recv()
+
+    sum_narrow(0)
+    pl.semaphore_wait(known.at[0], 3)
+    for d in (2, -2):
+        pl.semaphore_signal(known.at[1], inc=1, device_id=at_z(d), device_id_type=MESH)
+
+    def keep(which, spot, value):
+        hi, lo = split(value.T)
+        xt[which, 0, :, spot] = hi
+        xt[which, 1, :, spot] = lo
+
+    def keep_x(p):
+        for d in (1, 2, 3):
+            fx_copy(p, d).wait_recv()
+        keep(0, pl.ds(p * 256, 256), xg[:, p].reshape(256, 256))
 
     cpart[...] = dot(crossT, xg[x, 0])
-    pl.semaphore_wait(known, 3)
+    pl.semaphore_wait(known.at[1], 2)
 
     def rows_of(i):
         return pl.ds(pl.multiple_of(i * 8, 8), 8)
 
-    def rs_copy(i):
-        to = (w + i) % NW
-        return remote(
-            cpart.at[rows_of(to)], crecv.at[w], rs_s.at[i], rs_r.at[NW - i], (to, n)
-        )
-
-    def ag_copy(i):
-        return remote(
-            restall.at[rows_of(w)], restall.at[rows_of(w)], ag_s.at[i], ag_r.at[NW - i],
-            ((w + i) % NW, n),
+    def peer(j):
+        dz = (4 - (j // 4 + 1) // 2) * (1 - 2 * (j // 4 % 2))
+        q = j % 4
+        dx = 2 + (q + 1) // 2 * (1 - 2 * (q % 2))
+        return xpos(dx) * NZ + zpos(dz)
+
+    def rs_copy(j):
+        to = peer(j)
+        return remote(cpart.at[rows_of(to)], crecv.at[w], rs_s.at[j], rs_r.at[j], (to, n))
+
+    def ag_copy(j):
+        return remote(
+            restall.at[rows_of(w)], restall.at[rows_of(w)], ag_s.at[j], ag_r.at[j], (peer(j), n)
         )
 
     def each_peer(copy, act):
         def body(i, carry):
             act(copy(i))
             return carry
-        lax.fori_loop(1, NW, body, 0)
+        lax.fori_loop(0, NW - 1, body, 0)
 
     each_peer(rs_copy, start)
+    feed(3)
     crecv[w] = cpart[rows_of(w), :]
     each_peer(rs_copy, arrived)
     restall[rows_of(w), :] = pl_ref[1, rows_of(w), :] - jnp.sum(crecv[...], axis=0)
     each_peer(ag_copy, start)
+    feed(4)
+    pass_on(0)
+    sol_ref[0] = xg[x, 0]
+    keep_x(0)
     each_peer(ag_copy, arrived)
 
     part[1] = dot(inv_ref[1], restall[...])
-    sum_narrow(1, lambda stage: None)
-
-    for p in (0, 1):
-        for d in (1, 2, 3):
-            gx_copy(p, d).wait_recv()
+    sum_narrow(1)
+
+    def keep_z():
+        for p in (0, 1):
+            for i in range(4):
+                fz_copy(p, i).wait_recv()
+        around = [xg[x].reshape(128, 256), xz[0].reshape(128, 256), xz[1].reshape(128, 256)]
+        keep(1, pl.ds(0, 512), jnp.concatenate(around + [xz[2, 0], xz[3, 0]], axis=0))
+        keep(2, pl.ds(0, 512), jnp.concatenate(around + [xz[2, 1], xz[3, 1]], axis=0))
         for i in range(4):
-            gz_copy(p, i).wait_recv()
-
-    def keep(which, value):
-        hi, lo = split(value.T)
-        xt[which, 0] = hi
-        xt[which, 1] = lo
-
-    keep(0, xg[...].reshape(512, 256))
-    around = [xg[x].reshape(128, 256), xz[0].reshape(128, 256), xz[1].reshape(128, 256)]
-    keep(1, jnp.concatenate(around + [xz[2, 0], xz[3, 0]], axis=0))
-    keep(2, jnp.concatenate(around + [xz[2, 1], xz[3, 1]], axis=0))
-
-    for i in range(4):
-        each2(i, arrived)
-    for far in (0, 1):
-        for xd in range(NX):
-            own2(xd, far).wait()
+            each2(i, arrived)
+        for far in (0, 1):
+            for xd in range(NX):
+                own2(xd, far).wait()
 
     def product2(far):
         value = dot3(xt[1 + far, 0], xt[1 + far, 1], a2[far].reshape(512, NX * R2))
@@ -294,19 +356,24 @@
 
     def z_step(way, s):
         zd = zpos((-1, 1)[way] * (4 - s))
-        halves = (way, 1 - way) if s == 1 else (way, 1 - way)
+        halves = (1 - way, way) if s == 1 else (way, 1 - way)
         for h in halves:
             if s > 1 or h == way:
                 z_copy(way, s - 1, h).wait_recv()
                 pb[zd, H[h], :] = pb[zd, H[h], :] + recv1[way, s - 1, H[h], :]
             z_copy(way, s, h).start()
 
+    pass_on(1)
+    sol_ref[1] = xg[x, 1]
+    keep_x(1)
     product1(4)
     z_copy(0, 0, 0).start()
     z_copy(1, 0, 1).start()
+    keep_z()
     product2(1)
     for way in (0, 1):
         x_first(1, way).start()
+    feed(9)
     product1(-3)
     product1(3)
     z_step(0, 1)
@@ -316,6 +383,7 @@
         spot = xpos((1, -1)[way])
         qb[1, spot, H[way], :] = qb[1, spot, H[way], :] + xr0[1, way]
         x_second(1, way).start()
+    feed(10)
     product2(0)
     for way in (0, 1):
         x_first(0, way).start()
@@ -355,8 +423,10 @@
         for d in (1, 2, 3):
             y_copy(p, d).wait_send()
             gx_copy(p, d).wait_send()
+            fx_copy(p, d).wait_send()
         for i in range(4):
             gz_copy(p, i).wait_send()
+            fz_copy(p, i).wait_send()
     each_peer(rs_copy, sent)
     each_peer(ag_copy, sent)
     for d in (1, 2, 3):
@@ -380,6 +450,10 @@
     vmem = pl.BlockSpec(memory_space=pltpu.VMEM)
     dma = pltpu.SemaphoreType.DMA
     scratch = [
+        pltpu.VMEM((2, 256, 256), F32),
+        pltpu.VMEM((2, 64, 256), F32),
+        pltpu.VMEM((64, 256), F32),
+        pltpu.VMEM((ROWS, 256), F32),
         pltpu.VMEM((2, 64, 256), F32),
         pltpu.VMEM((2, 32, 256), F32),
         pltpu.VMEM((2, NY, 32, 256), F32),
@@ -388,7 +462,7 @@
         pltpu.VMEM((256, 256), F32),
         pltpu.VMEM((NW, 8, 256), F32),
         pltpu.VMEM((256, 256), F32),
-        pltpu.VMEM((NZ, NX, 2, 64, R1), F32),
+        pltpu.VMEM((NZ, 2, NX, 64, R1), F32),
         pltpu.VMEM((2, 4, 2, 64, NX * R2), F32),
         pltpu.VMEM((NZ, 256, R1), F32),
         pltpu.VMEM((2, NX, 256, R2), F32),
@@ -399,12 +473,13 @@
         pltpu.VMEM((256, R2), F32),
         pltpu.VMEM((3, 2, 256, 512), BF16),
         dma((2,)), dma((2,)), dma((2, 4)), dma((2, 4)), dma((2,)), dma((2,)),
-        pltpu.SemaphoreType.REGULAR,
+        pltpu.SemaphoreType.REGULAR((2,)),
         dma((NW,)), dma((NW,)), dma((NW,)), dma((NW,)),
+        dma((2, 4)), dma((2, 4)), dma((2, 4)), dma((2, 4)),
         dma((2, 4)), dma((2, 4)), dma((2, 4)), dma((2, 4)),
         dma((4, NZ)), dma((4, NZ)), dma((NZ,)),
         dma((4, 2, NX)), dma((4, 2, NX)), dma((2, NX)),
-        dma((2, 4, 2)), dma((2, 4, 2)), dma((2, 2, 2)), dma((2, 2, 2)), dma((1,)), dma((1,)),
+        dma((2, 4, 2)), dma((2, 4, 2)), dma((2, 2, 2)), dma((2, 2, 2)), dma((1,)), dma((1,)), dma((4,)),
     ]
     return pl.pallas_call(
         kernel,
@@ -412,11 +487,11 @@
             jax.ShapeDtypeStruct((2, 64, 256), F32),
             jax.ShapeDtypeStruct((ROWS, 256), F32),
         ),
-        in_specs=[vmem, vmem, vmem, vmem, pl.BlockSpec(memory_space=pl.ANY)],
+        in_specs=[pl.BlockSpec(memory_space=pl.ANY)] * 5,
         out_specs=(vmem, vmem),
         scratch_shapes=scratch,
         compiler_params=pltpu.CompilerParams(
-            collective_id=0, has_side_effects=True, vmem_limit_bytes=48 * 1024 * 1024
+            collective_id=0, has_side_effects=True, vmem_limit_bytes=56 * 1024 * 1024
         ),
     )(panel_loads, inverses, cross_factor, tail_loads, tail_factor)
 

time: 125 us -> 91.6 us (0.73)
  Pallas kernels: 118 us -> 87.4 us
  local copies, waits for them, and re-layouts: 5.18 us -> 3.33 us
    pallas_call x1, Pallas kernels: 118 us -> 87.4 us  [on_device(): pl.pallas_call(kernel, out_shape=(jax.ShapeDtypeStruct((2, 64, 256), F32)...]
    unnamed x10 -> x2, local copies, waits for them, and re-layouts: 5.18 us -> 3.33 us
where the time goes in v2:
time: 91.6 us; the launch traced here: 91.4 us
  Pallas kernels  87.4 us (95%)
  local copies, waits for them, and re-layouts  3.33 us (4%)
    pallas_call x1, Pallas kernels, on_device(): pl.pallas_call(kernel, out_shape=(jax.ShapeDtypeStruct((2, 64, 256), F32)...  87.4 us
    unnamed x2, local copies, waits for them, and re-layouts  3.33 us

profile of v2, /device:TPU:1, one launch (start us, length us, event | category | flops | bytes accessed | tf_op | source)
XLA Modules:
  0.0 91.4 jit_solution(2618143047775714911)
XLA Ops:
  0.6 87.4 %shard_map.68 = (f32[2,64,256]{2,1,0:T(8,128)}, f32[384,256]{1,0:T(8,128)}) custom-call(f32[2,256,256]{2,1,0:T(8,128)} %pl_hbm.1, f32[2,64,256]{2,1,0:T(8,128)} %inv_hbm.1, f32[64,256]{1,0:T(8,128)} %cross_hbm.1, f32[384,256]{1,0:T(8,128)} %loads_hbm.1, f32[2,64,12288]{2,1,0:T(8,128)} %tail_ref.1), custom_call_target="tpu_custom_call" | custom-call | tf_op jit(solution)/shard_map/pallas_call | solution.py:484
  88.1 1.6 %copy.9 = f32[2,64,256]{2,1,0:T(8,128)} copy(f32[2,64,256]{2,1,0:T(8,128)} %get-tuple-element.4) | data formatting | bytes 262144
  89.6 1.8 %copy.10 = f32[384,256]{1,0:T(8,128)} copy(f32[384,256]{1,0:T(8,128)} %get-tuple-element.5) | data formatting | bytes 786432

commit v3 on v2

--- a/solution.py
+++ b/solution.py
@@ -17,13 +17,13 @@
 F32 = jnp.float32
 BF16 = jnp.bfloat16
 SCHEDULE = {
-    0: ((1, 0, 1),),
-    1: ((1, 1, 2), (2, 0, 1)),
+    0: ((1, 0, 1), (2, 0, 1)),
+    1: ((1, 1, 2),),
     2: (),
     3: ((1, 2, 3), (2, 1, 2)),
     4: ((1, 3, 4), (2, 2, 3)),
-    6: (),
-    7: ((1, 4, 5), (2, 3, 4)),
+    6: ((2, 3, 4),),
+    7: ((1, 4, 5),),
     8: ((1, 5, 6),),
     9: ((1, 6, 7),),
     10: ((1, 7, 8),),
@@ -121,7 +121,7 @@
     def send1(d, zd):
         return remote(
             tail_ref.at[:, :, lanes1(xpos(d), zd)], a1.at[zd, :, x],
-            a1_s.at[d, zd], a1_r.at[4 - d, zd], at_x(d),
+            a1_s.at[0], a1_r.at[zd], at_x(d),
         )
 
     def send2(i, xd, far):
@@ -134,7 +134,7 @@
         else:
             src = tail_ref.at[far, :, lanes2(xd, zd)]
             dst = a2.at[far, 3, i - 2, :, to]
-        return remote(src, dst, a2_s.at[i, far, xd], a2_r.at[i, far, xd], at_z(d))
+        return remote(src, dst, a2_s.at[0], a2_r.at[0], at_z(d))
 
     def feed1(first, last):
         def body(i, carry):
@@ -158,22 +158,8 @@
         for kind, first, last in SCHEDULE[stage]:
             (feed1 if kind == 1 else feed2)(first, last)
 
-    def each1(d, act):
-        def body(zd, carry):
-            act(send1(d, zd))
-            return carry
-        lax.fori_loop(0, NZ, body, 0)
-
-    def each2(i, act):
-        def body(xd, carry):
-            for far in (0, 1):
-                act(send2(i, xd, far))
-            return carry
-        lax.fori_loop(0, NX, body, 0)
-
-    start = lambda copy: copy.start()
-    sent = lambda copy: copy.wait_send()
-    arrived = lambda copy: copy.wait_recv()
+    def whole(like, sem):
+        pltpu.make_async_copy(like, like, sem).wait()
 
     for copy in loads:
         copy.wait()
@@ -238,6 +224,12 @@
         ybuf[p, y] = part[p, mine] + corebuf[p]
         for d in (2, 1, 3):
             y_copy(p, d).start()
+        if p == 0:
+            pl.semaphore_wait(known.at[0], 3)
+            for d in (2, -2):
+                pl.semaphore_signal(
+                    known.at[1], inc=1, device_id=at_z(d), device_id_type=MESH
+                )
         feed(6 * p + 1)
         for d in (2, 1, 3):
             y_copy(p, d).wait_recv()
@@ -251,9 +243,6 @@
         cg_copy(p).wait_recv()
 
     sum_narrow(0)
-    pl.semaphore_wait(known.at[0], 3)
-    for d in (2, -2):
-        pl.semaphore_signal(known.at[1], inc=1, device_id=at_z(d), device_id_type=MESH)
 
     def keep(which, spot, value):
         hi, lo = split(value.T)
@@ -279,30 +268,30 @@
 
     def rs_copy(j):
         to = peer(j)
-        return remote(cpart.at[rows_of(to)], crecv.at[w], rs_s.at[j], rs_r.at[j], (to, n))
+        return remote(cpart.at[rows_of(to)], crecv.at[w], rs_s.at[0], rs_r.at[0], (to, n))
 
     def ag_copy(j):
         return remote(
-            restall.at[rows_of(w)], restall.at[rows_of(w)], ag_s.at[j], ag_r.at[j], (peer(j), n)
-        )
-
-    def each_peer(copy, act):
-        def body(i, carry):
-            act(copy(i))
+            restall.at[rows_of(w)], restall.at[rows_of(w)], ag_s.at[0], ag_r.at[0], (peer(j), n)
+        )
+
+    def to_peers(copy):
+        def body(j, carry):
+            copy(j).start()
             return carry
         lax.fori_loop(0, NW - 1, body, 0)
 
-    each_peer(rs_copy, start)
+    to_peers(rs_copy)
     feed(3)
     crecv[w] = cpart[rows_of(w), :]
-    each_peer(rs_copy, arrived)
+    whole(crecv.at[pl.ds(0, NW - 1)], rs_r.at[0])
     restall[rows_of(w), :] = pl_ref[1, rows_of(w), :] - jnp.sum(crecv[...], axis=0)
-    each_peer(ag_copy, start)
+    to_peers(ag_copy)
     feed(4)
     pass_on(0)
     sol_ref[0] = xg[x, 0]
     keep_x(0)
-    each_peer(ag_copy, arrived)
+    whole(restall.at[pl.ds(0, 8 * (NW - 1))], ag_r.at[0])
 
     part[1] = dot(inv_ref[1], restall[...])
     sum_narrow(1)
@@ -314,8 +303,7 @@
         around = [xg[x].reshape(128, 256), xz[0].reshape(128, 256), xz[1].reshape(128, 256)]
         keep(1, pl.ds(0, 512), jnp.concatenate(around + [xz[2, 0], xz[3, 0]], axis=0))
         keep(2, pl.ds(0, 512), jnp.concatenate(around + [xz[2, 1], xz[3, 1]], axis=0))
-        for i in range(4):
-            each2(i, arrived)
+        whole(a2.at[:, pl.ds(0, 3)], a2_r.at[0])
         for far in (0, 1):
             for xd in range(NX):
                 own2(xd, far).wait()
@@ -350,8 +338,7 @@
     def product1(d):
         zd = zpos(d)
         own1(zd).wait()
-        for k in (1, 2, 3):
-            send1(k, zd).wait_recv()
+        whole(a1.at[zd, :, pl.ds(0, NX - 1)], a1_r.at[zd])
         pb[zd] = dot3(xt[0, 0], xt[0, 1], a1[zd].reshape(512, R1))
 
     def z_step(way, s):
@@ -406,17 +393,6 @@
     z_step(0, 3)
     z_step(1, 3)
     product1(0)
-    for way in (0, 1):
-        x_second(0, way).wait_recv()
-    far_copy.wait_recv()
-    total2 = qb[0, x] + (xr1[0, 0] + xr1[0, 1]) + farrecv[...]
-    out_ref[R1:, :] = loads_ref[R1:, :] - total2.T
-    for way in (0, 1):
-        for h in (0, 1):
-            z_copy(way, 3, h).wait_recv()
-    total1 = pb[z] + (recv1[0, 3] + recv1[1, 3])
-    out_ref[:R1, :] = loads_ref[:R1, :] - total1.T
-
     for p in (0, 1):
         core_copy(p).wait_send()
         cg_copy(p).wait_send()
@@ -427,12 +403,21 @@
         for i in range(4):
             gz_copy(p, i).wait_send()
             fz_copy(p, i).wait_send()
-    each_peer(rs_copy, sent)
-    each_peer(ag_copy, sent)
-    for d in (1, 2, 3):
-        each1(d, sent)
-    for i in range(4):
-        each2(i, sent)
+    whole(crecv.at[pl.ds(0, NW - 1)], rs_s.at[0])
+    whole(restall.at[pl.ds(0, 8 * (NW - 1))], ag_s.at[0])
+    whole(a2.at[:, pl.ds(0, 3)], a2_s.at[0])
+    for way in (0, 1):
+        x_second(0, way).wait_recv()
+    far_copy.wait_recv()
+    total2 = qb[0, x] + (xr1[0, 0] + xr1[0, 1]) + farrecv[...]
+    out_ref[R1:, :] = loads_ref[R1:, :] - total2.T
+    for way in (0, 1):
+        for h in (0, 1):
+            z_copy(way, 3, h).wait_recv()
+    total1 = pb[z] + (recv1[0, 3] + recv1[1, 3])
+    out_ref[:R1, :] = loads_ref[:R1, :] - total1.T
+
+    whole(a1.at[pl.ds(0, 6)], a1_s.at[0])
     for far in (0, 1):
         for way in (0, 1):
             x_first(far, way).wait_send()
@@ -474,11 +459,11 @@
         pltpu.VMEM((3, 2, 256, 512), BF16),
         dma((2,)), dma((2,)), dma((2, 4)), dma((2, 4)), dma((2,)), dma((2,)),
         pltpu.SemaphoreType.REGULAR((2,)),
-        dma((NW,)), dma((NW,)), dma((NW,)), dma((NW,)),
+        dma((1,)), dma((1,)), dma((1,)), dma((1,)),
         dma((2, 4)), dma((2, 4)), dma((2, 4)), dma((2, 4)),
         dma((2, 4)), dma((2, 4)), dma((2, 4)), dma((2, 4)),
-        dma((4, NZ)), dma((4, NZ)), dma((NZ,)),
-        dma((4, 2, NX)), dma((4, 2, NX)), dma((2, NX)),
+        dma((1,)), dma((NZ,)), dma((NZ,)),
+        dma((1,)), dma((1,)), dma((2, NX)),
         dma((2, 4, 2)), dma((2, 4, 2)), dma((2, 2, 2)), dma((2, 2, 2)), dma((1,)), dma((1,)), dma((4,)),
     ]
     return pl.pallas_call(

time: 91.6 us -> 87.1 us (0.951)
  Pallas kernels: 87.4 us -> 83 us
    pallas_call x1, Pallas kernels: 87.4 us -> 83 us  [on_device(): pl.pallas_call(kernel, out_shape=(jax.ShapeDtypeStruct((2, 64, 256), F32)...]
where the time goes in v3:
time: 87.1 us; the launch traced here: 87 us
  Pallas kernels  83 us (95%)
  local copies, waits for them, and re-layouts  3.33 us (4%)
    pallas_call x1, Pallas kernels, on_device(): pl.pallas_call(kernel, out_shape=(jax.ShapeDtypeStruct((2, 64, 256), F32)...  83 us
    unnamed x2, local copies, waits for them, and re-layouts  3.33 us

profile of v3, /device:TPU:1, one launch (start us, length us, event | category | flops | bytes accessed | tf_op | source)
XLA Modules:
  0.0 87.0 jit_solution(18229935790017231983)
XLA Ops:
  0.6 83.0 %shard_map.68 = (f32[2,64,256]{2,1,0:T(8,128)}, f32[384,256]{1,0:T(8,128)}) custom-call(f32[2,256,256]{2,1,0:T(8,128)} %pl_hbm.1, f32[2,64,256]{2,1,0:T(8,128)} %inv_hbm.1, f32[64,256]{1,0:T(8,128)} %cross_hbm.1, f32[384,256]{1,0:T(8,128)} %loads_hbm.1, f32[2,64,12288]{2,1,0:T(8,128)} %tail_ref.1), custom_call_target="tpu_custom_call" | custom-call | tf_op jit(solution)/shard_map/pallas_call | solution.py:469
  83.6 1.6 %copy.9 = f32[2,64,256]{2,1,0:T(8,128)} copy(f32[2,64,256]{2,1,0:T(8,128)} %get-tuple-element.4) | data formatting | bytes 262144
  85.2 1.8 %copy.10 = f32[384,256]{1,0:T(8,128)} copy(f32[384,256]{1,0:T(8,128)} %get-tuple-element.5) | data formatting | bytes 786432

commit v4 on v3

--- a/solution.py
+++ b/solution.py
@@ -360,9 +360,9 @@
     product2(1)
     for way in (0, 1):
         x_first(1, way).start()
-    feed(9)
     product1(-3)
     product1(3)
+    feed(9)
     z_step(0, 1)
     z_step(1, 1)
     for way in (0, 1):

time: 87.1 us -> 88.6 us (1.017)
  Pallas kernels: 83 us -> 84.5 us
    pallas_call x1, Pallas kernels: 83 us -> 84.5 us  [on_device(): pl.pallas_call(kernel, out_shape=(jax.ShapeDtypeStruct((2, 64, 256), F32)...]
where the time goes in v4:
time: 88.6 us; the launch traced here: 88.5 us
  Pallas kernels  84.5 us (95%)
  local copies, waits for them, and re-layouts  3.33 us (4%)
    pallas_call x1, Pallas kernels, on_device(): pl.pallas_call(kernel, out_shape=(jax.ShapeDtypeStruct((2, 64, 256), F32)...  84.5 us
    unnamed x2, local copies, waits for them, and re-layouts  3.33 us

profile of v4, /device:TPU:1, one launch (start us, length us, event | category | flops | bytes accessed | tf_op | source)
XLA Modules:
  0.0 88.5 jit_solution(1327939283768838836)
XLA Ops:
  0.6 84.5 %shard_map.68 = (f32[2,64,256]{2,1,0:T(8,128)}, f32[384,256]{1,0:T(8,128)}) custom-call(f32[2,256,256]{2,1,0:T(8,128)} %pl_hbm.1, f32[2,64,256]{2,1,0:T(8,128)} %inv_hbm.1, f32[64,256]{1,0:T(8,128)} %cross_hbm.1, f32[384,256]{1,0:T(8,128)} %loads_hbm.1, f32[2,64,12288]{2,1,0:T(8,128)} %tail_ref.1), custom_call_target="tpu_custom_call" | custom-call | tf_op jit(solution)/shard_map/pallas_call | solution.py:469
  85.1 1.6 %copy.9 = f32[2,64,256]{2,1,0:T(8,128)} copy(f32[2,64,256]{2,1,0:T(8,128)} %get-tuple-element.4) | data formatting | bytes 262144
  86.7 1.8 %copy.10 = f32[384,256]{1,0:T(8,128)} copy(f32[384,256]{1,0:T(8,128)} %get-tuple-element.5) | data formatting | bytes 786432
